TPU v7x, 32 devices: a whole 2x2x4 slice. The times are simulated.
32 devices in a mesh: slab: 2 (over y), date: 4 (over z), rng: 2 (over x), az: 2 (over core).
Axes of the slice: x: 2, y: 2, z: 4, core: 2. Of those that a mesh axis runs over, the one named last changes fastest.
Arguments:
- slc: bfloat16 [64, 2, 128, 512], P(('slab', 'date'), None, 'az', 'rng'), parts along dimension 0, may hold values from -30 to 30
- lags: int32 [32, 6], P('date'), may hold values from 0 to 8, as said below
Outputs:
- coherence: bfloat16 [64, 6, 128, 512], P(('slab', 'date'), None, 'az', 'rng'), parts along dimension 0
- log_ratio: bfloat16 [64, 6, 128, 512], P(('slab', 'date'), None, 'az', 'rng'), parts along dimension 0
- quegan: float32 [64, 128, 512], P(('slab', 'date'), 'az', 'rng'), parts along dimension 0
There are 2 independent parts, one for each index of `slab`. A program takes and returns all parts, laid end to end along the dimension named above; an argument that names none is the same for every part. Nothing has to cross between parts.
Inputs may be any that keep to these rules, and one draw needn't show every extreme that they name: Each entry is 0 (no partner) or a lag with date + lag < 32; the nonzero lags of one date are distinct; date 0 lists 6 partners, one of them at lag 8.
All inputs are finite; a program needn't handle non-finite values.
Results may differ from a plain program's by a relative error of at most 0.012.
Values may be sent and summed in bfloat16 or wider, within the bound.
No kernel may reach another device: no remote copies, remote signals or barrier semaphores. Data moves between devices by JAX's collectives and lax.ppermute only.
A program may use at most 64 MiB of HBM per device.

v0:
```python
import jax
import jax.numpy as jnp
from jax import lax
from jax.experimental import pallas as pl
from jax.experimental.pallas import tpu as pltpu
from jax.sharding import PartitionSpec as P

HALF_AZ = 2
HALF_RG = 10
EPS = 1e-05
LOOKS = float((2 * HALF_AZ + 1) * (2 * HALF_RG + 1))

BF16 = jnp.bfloat16
F32 = jnp.float32
STRIP = 16
LANES = 128
GROUP = 4
ENDS = (3, 5)
PARTS = 1


def sides(axis, size, width):
    count = lax.axis_size(axis)
    me = lax.axis_index(axis)
    if count == 2:
        first = me == 0
        return [(jnp.where(first, size - width, 0), jnp.where(first, size, -width), [(0, 1), (1, 0)])]
    return [
        (size - width, -width, [(i, i + 1) for i in range(count - 1)]),
        (0, size, [(i + 1, i) for i in range(count - 1)]),
    ]


def marks(shape, where):
    row = lax.broadcasted_iota(jnp.int32, shape, 0)
    col = lax.broadcasted_iota(jnp.int32, shape, 1)
    return jnp.where(where(row, col), 1.0, 0.0).astype(BF16)


def dot(a, b, contract=(1, 0)):
    return lax.dot_general(a, b, (((contract[0],), (contract[1],)), ((), ())), preferred_element_type=F32)


class Sizes:
    def __init__(self, slc, lags):
        self.dates, _, self.lines, self.cols = slc.shape
        self.slots = lags.shape[1]
        self.images = 2 * self.dates
        self.az = 1 if lax.axis_size("az") == 2 else 2
        self.rng = 1 if lax.axis_size("rng") == 2 else 2
        self.rows = self.lines + STRIP
        self.width = self.cols + LANES
        self.slot_count = self.dates * self.slots
        self.ends = tuple((self.dates * n) // 8 for n in ENDS)
        self.rim_rows = 0
        self.rim_cols = self.az * HALF_AZ * self.cols
        self.rim_corners = self.rim_cols + self.rng * self.images * self.lines
        self.rim_width = self.rim_corners + self.az * self.rng * LANES


def make_lists(z, lags_ref, lists_ref, count_ref):
    for n in range(3):
        count_ref[n] = 0
    for d in range(z.dates):
        for s in range(z.slots):
            lag = lags_ref[d, s]
            which = jnp.where(lag > 0, jnp.where(d + lag < z.dates, 1, 2), 0)
            at = count_ref[which]
            lists_ref[which, at] = d * 65536 + s * 256 + d + lag
            count_ref[which] = at + 1
    for n in range(3):
        lists_ref[n, z.slot_count] = count_ref[n]


def places(z, axis, k, inside, tail, unit, width):
    at = jnp.where(k < inside, k, -(10**6))
    for j, (_, place, _) in enumerate(sides(axis, inside, width)):
        c = k - tail - j * unit
        at = jnp.where((c >= 0) & (c < width), place + c, at)
    return at


def near(a, b, reach):
    return jnp.where(jnp.abs(a - b) <= reach, 1.0, 0.0).astype(BF16)


def make_bands(z, columns_ref):
    at = places(z, "rng", lax.broadcasted_iota(jnp.int32, (z.width, 1), 0), z.cols, z.cols, STRIP, HALF_RG)
    columns_ref[...] = near(at, lax.broadcasted_iota(jnp.int32, (z.width, z.cols), 1), HALF_RG)


def pack_kernel(z, slc_ref, *out):
    held_ref, sems = out[z.az + z.rng + z.az * z.rng :]
    part = z.images * z.lines // PARTS
    copies = [
        pltpu.make_async_copy(slc_ref.at[pl.ds(n * part, part)], held_ref.at[pl.ds(n * part, part)], sems.at[n])
        for n in range(PARTS)
    ]
    for copy in copies:
        copy.start()
    az, rng = sides("az", z.lines, HALF_AZ), sides("rng", z.cols, HALF_RG)
    picks, lanes = [], []
    for start, _, _ in rng:
        low = pl.multiple_of(jnp.where(start == 0, 0, z.cols - LANES), LANES)
        lanes.append(pl.ds(low, LANES))
        picks.append(marks((STRIP, LANES), lambda c, k: (k == start - low + c) & (c < HALF_RG)))
    for n, copy in enumerate(copies):
        copy.wait()
        for j, pick in enumerate(picks):
            columns = held_ref[n * part : (n + 1) * part, lanes[j]]
            out[z.az + j][:, n * part : (n + 1) * part] = dot(pick, columns, (1, 1)).astype(BF16)
    q = lax.broadcasted_iota(jnp.int32, (LANES, 1), 0)
    for i, (start, _, _) in enumerate(az):
        low = jnp.where(start == 0, 0, z.lines - STRIP)
        rows = [held_ref[pl.ds(pl.multiple_of(m * z.lines + low, STRIP), STRIP), :] for m in range(z.images)]
        wanted = jnp.where(q < HALF_AZ * z.images, (q % z.images) * STRIP + start - low + q // z.images, -1)
        put = near(wanted, lax.broadcasted_iota(jnp.int32, (LANES, z.images * STRIP), 1), 0)
        edge = dot(put, jnp.concatenate(rows, axis=0)).astype(BF16)
        for r in range(HALF_AZ):
            out[i][:, r * z.cols : (r + 1) * z.cols] = edge[r * z.images : (r + 1) * z.images]
        for j, (first, _, _) in enumerate(rng):
            pick = marks((STRIP, z.cols), lambda c, k: (k == first + c) & (c < HALF_RG))
            out[z.az + z.rng + i * z.rng + j][...] = dot(pick, edge, (1, 1)).astype(BF16)


def prepare_kernel(z, lags_ref, columns_ref, lists_ref, lags_s, lists_s, count_s, sem):
    take = pltpu.make_async_copy(lags_ref, lags_s, sem)
    take.start()
    make_bands(z, columns_ref)
    take.wait()
    make_lists(z, lags_s, lists_s, count_s)
    give = pltpu.make_async_copy(lists_s, lists_ref, sem)
    give.start()
    give.wait()


def assemble(z, tile_ref, x_ref, rim_ref, first, number):
    tile_ref[:, STRIP:, : z.cols] = x_ref[...].reshape(number, z.lines, z.cols)
    p = lax.broadcasted_iota(jnp.int32, (number * STRIP, 1), 0)
    az = [jnp.where(place < 0, STRIP + place, 0) for _, place, _ in sides("az", z.lines, HALF_AZ)]
    edge = jnp.zeros((number * STRIP, z.cols), F32)
    for i in range(z.az):
        for r in range(HALF_AZ):
            wanted = jnp.where(p % STRIP == az[i] + r, first + p // STRIP, -1)
            put = near(wanted, lax.broadcasted_iota(jnp.int32, (number * STRIP, z.images), 1), 0)
            at = (i * HALF_AZ + r) * z.cols
            edge = edge + dot(put, rim_ref[: z.images, at : at + z.cols])
    tile_ref[:, :STRIP, : z.cols] = edge.astype(BF16).reshape(number, STRIP, z.cols)
    side = jnp.zeros((number * z.lines, LANES), F32)
    corner = jnp.zeros((number * STRIP, LANES), F32)
    for j in range(z.rng):
        spread = marks((STRIP, LANES), lambda c, lane: lane == c + j * STRIP)
        at = z.rim_cols + (j * z.images + first) * z.lines
        side = side + dot(rim_ref[:STRIP, at : at + number * z.lines], spread, (0, 0))
        for i in range(z.az):
            at = z.rim_corners + (i * z.rng + j) * LANES
            turned = dot(rim_ref[:STRIP, at : at + LANES], spread, (0, 0)).astype(BF16)
            r = p % STRIP - az[i]
            wanted = jnp.where((r >= 0) & (r < HALF_AZ), r * z.images + first + p // STRIP, -1)
            put = near(wanted, lax.broadcasted_iota(jnp.int32, (number * STRIP, LANES), 1), 0)
            corner = corner + dot(put, turned)
    tile_ref[:, STRIP:, z.cols :] = side.astype(BF16).reshape(number, z.lines, LANES)
    tile_ref[:, :STRIP, z.cols :] = corner.astype(BF16).reshape(number, STRIP, LANES)


def split(x):
    high = x.astype(BF16)
    return high, (x - high.astype(F32)).astype(BF16)


def down_sums(z, x):
    half = STRIP // 2
    x = jnp.concatenate([x[half:], x[:half]], axis=0)
    top = half - HALF_AZ
    twos = x[top : top + z.lines + 3] + x[top + 1 : top + z.lines + 4]
    fours = twos[: z.lines + 1] + twos[2 : z.lines + 3]
    return fours[: z.lines] + x[half + HALF_AZ : half + HALF_AZ + z.lines]


def look_stats(z, tile, first, number, columns):
    powers, parts = [], []
    for d in range(first, first + number):
        re, im = tile[2 * d].astype(F32), tile[2 * d + 1].astype(F32)
        power = re * re + im * im
        powers.append(power[STRIP:, : z.cols])
        parts += split(power)
    sums = dot(jnp.concatenate(parts, axis=0), columns)
    for n, power in enumerate(powers):
        at = 2 * n * z.rows
        both = sums[at : at + z.rows] + sums[at + z.rows : at + 2 * z.rows]
        mean = down_sums(z, both) * (1.0 / LOOKS) + EPS
        yield first + n, power, mean, 1.0 / mean


def stats_kernel(z, x_ref, rim_ref, columns, tile_ref, mean_ref, inv_ref, log_ref, part_ref, bundle_ref):
    assemble(z, tile_ref, x_ref, rim_ref, 0, z.images)
    part = jnp.zeros((z.lines, z.cols), F32)
    for first in range(0, z.dates, GROUP):
        for d, power, mean, inv in look_stats(z, tile_ref, first, min(GROUP, z.dates - first), columns[...]):
            mean_ref[d] = mean
            inv_ref[d] = inv * (1.0 / LOOKS)
            log_ref[d] = jnp.log(mean)
            part = part + power * inv
    part = part.astype(BF16)
    part_ref[...] = part
    bundle_ref[:, : z.rim_width] = rim_ref[...]
    for i in range(z.lines // STRIP):
        at = z.rim_width + i * z.cols
        bundle_ref[:STRIP, at : at + z.cols] = part[i * STRIP : (i + 1) * STRIP]


def do_pairs(z, own, other, first_other, own_inv, own_log, other_inv, other_log, columns, lists, row, coh, log, emit=None):
    count = lists[row, z.slot_count]

    def pick(k):
        code = lists[row, jnp.minimum(k, count - 1)]
        return code // 65536, (code // 256) % 256, code % 256 - first_other

    def group(step, sent):
        picks = [pick(step * GROUP + g) for g in range(GROUP)]
        products = []
        for d, _, e in picks:
            a0, a1, b0, b1 = own[2 * d], own[2 * d + 1], other[2 * e], other[2 * e + 1]
            products += [a0 * b0 + a1 * b1, a1 * b0 - a0 * b1]
        sums = dot(jnp.concatenate(products, axis=0), columns)
        for g, (d, s, e) in enumerate(picks):
            at = 2 * g * z.rows
            re = down_sums(z, sums[at : at + z.rows])
            im = down_sums(z, sums[at + z.rows : at + 2 * z.rows])
            coh[d, s] = ((re * re + im * im) * (own_inv[d] * other_inv[e])).astype(BF16)
            log[d, s] = (own_log[d] - other_log[e]).astype(BF16)
        if emit is None:
            return sent
        following = (step + 1) * GROUP
        ready = jnp.where(following < count, pick(following)[0], z.dates)
        emit(sent, ready)
        return ready

    sent = lax.fori_loop(0, (count + GROUP - 1) // GROUP, group, 0)
    if emit is not None:
        emit(sent, z.dates)


def own_kernel(z, lists_ref, columns, tile, inv, log, coh, logr, lists, sem):
    take = pltpu.make_async_copy(lists_ref, lists, sem)
    take.start()
    take.wait()
    empty = jnp.zeros((z.lines, z.cols), BF16)

    def clear(k, _):
        code = lists[0, k]
        d, s = code // 65536, (code // 256) % 256
        coh[d, s] = empty
        logr[d, s] = empty
        return 0

    lax.fori_loop(0, lists[0, z.slot_count], clear, 0)
    do_pairs(z, tile, tile, 0, inv, log, inv, log, columns[...], lists, 1, coh, logr)


def cross_kernel(z, x_ref, rim_ref, lists_ref, columns, own, own_inv, own_log, coh_in, log_in, coh_out, log_out, coh_last, log_last, tile, inv, log, lists, coh, logr, sems):
    takes = [
        pltpu.make_async_copy(lists_ref, lists, sems.at[0]),
        pltpu.make_async_copy(coh_in, coh, sems.at[1]),
        pltpu.make_async_copy(log_in, logr, sems.at[2]),
    ]
    for take in takes:
        take.start()
    assemble(z, tile, x_ref, rim_ref, 0, z.images)
    for first in range(0, z.dates, GROUP):
        for d, _, mean, inverse in look_stats(z, tile, first, min(GROUP, z.dates - first), columns[...]):
            inv[d] = inverse * (1.0 / LOOKS)
            log[d] = jnp.log(mean)
    for take in takes:
        take.wait()

    spans = [(low, high - low) for low, high in zip((0,) + z.ends, z.ends)]

    def copies(low, number):
        span = pl.ds(low, number)
        return (
            pltpu.make_async_copy(coh.at[span], coh_out.at[span], sems.at[3]),
            pltpu.make_async_copy(logr.at[span], log_out.at[span], sems.at[3]),
        )

    def emit(sent, ready):
        for low, number in spans:

            @pl.when((sent < low + number) & (ready >= low + number))
            def _():
                for copy in copies(low, number):
                    copy.start()

    do_pairs(z, own, tile, z.dates, own_inv, own_log, inv, log, columns[...], lists, 2, coh, logr, emit)
    coh_last[...] = coh[z.ends[-1] :]
    log_last[...] = logr[z.ends[-1] :]
    for low, number in spans:
        for copy in copies(low, number):
            copy.wait()


def quegan_kernel(z, dates_total, rotated, coh_in, log_in, coh_last, log_last, mean, rim_ref, *refs):
    parts, (coh_out, log_out, out, stage, sems) = refs[:-5], refs[-5:]
    span = pl.ds(z.ends[-1], z.dates - z.ends[-1])
    copies = [
        pltpu.make_async_copy(coh_last, coh_out.at[span], sems.at[0]),
        pltpu.make_async_copy(log_last, log_out.at[span], sems.at[1]),
        pltpu.make_async_copy(stage, out, sems.at[2]),
    ]
    for copy in copies[:2]:
        copy.start()
    total = parts[0][...].astype(F32)
    for part in parts[1:]:
        total = total + part[...].astype(F32)
    if rotated:
        ats = [z.rim_width + i * z.cols for i in range(z.lines // STRIP)]
        total = total + jnp.concatenate([rim_ref[:STRIP, at : at + z.cols] for at in ats], axis=0).astype(F32)
    total = total * (1.0 / dates_total)
    for d in range(z.dates):
        stage[d] = mean[d] * total
    copies[2].start()
    for copy in copies:
        copy.wait()


def vmem(n):
    return [pl.BlockSpec(memory_space=pltpu.VMEM)] * n


SMEM = pl.BlockSpec(memory_space=pltpu.SMEM)
HBM = pl.BlockSpec(memory_space=pltpu.HBM)
PARAMS = pltpu.CompilerParams(vmem_limit_bytes=32 * 1024 * 1024)
COST = pl.CostEstimate(flops=1, bytes_accessed=1, transcendentals=0)


def on_device(slc, lags):
    z = Sizes(slc, lags)
    shape = jax.ShapeDtypeStruct
    flat = slc.reshape(z.images * z.lines, z.cols)
    count = lax.axis_size("date")
    earlier = [(i, i - 1) for i in range(1, count)]
    later = lax.ppermute(flat, "date", earlier)
    packed = pl.pallas_call(
        lambda *refs: pack_kernel(z, *refs),
        out_shape=[shape((STRIP, HALF_AZ * z.cols), BF16)] * z.az
        + [shape((STRIP, z.images * z.lines), BF16)] * z.rng
        + [shape((STRIP, LANES), BF16)] * (z.az * z.rng)
        + [shape(flat.shape, BF16)],
        in_specs=[HBM],
        out_specs=vmem(z.az + z.rng + z.az * z.rng + 1),
        scratch_shapes=[pltpu.SemaphoreType.DMA((PARTS,))],
        compiler_params=PARAMS,
        cost_estimate=COST,
        name="pack",
    )(pltpu.with_memory_space_constraint(flat, pltpu.HBM))
    held = packed[-1]
    az, rng = sides("az", z.lines, HALF_AZ), sides("rng", z.cols, HALF_RG)

    lists_shape = (3, z.slot_count + 1)
    own_lists = pltpu.SMEM(lists_shape, jnp.int32)
    rim = [lax.ppermute(packed[i], "az", az[i][2]) for i in range(z.az)]
    lags, _ = lax.optimization_barrier((lags, packed[0]))
    columns, lists = pl.pallas_call(
        lambda *refs: prepare_kernel(z, *refs),
        out_shape=[shape((z.width, z.cols), BF16), shape(lists_shape, jnp.int32)],
        in_specs=[HBM],
        out_specs=vmem(2),
        scratch_shapes=[pltpu.SMEM(lags.shape, jnp.int32), own_lists, pltpu.SMEM((3,), jnp.int32)]
        + [pltpu.SemaphoreType.DMA],
        compiler_params=PARAMS,
        cost_estimate=COST,
        name="prepare",
    )(pltpu.with_memory_space_constraint(lags, pltpu.HBM))
    rim += [lax.ppermute(packed[z.az + j], "rng", rng[j][2]) for j in range(z.rng)]
    az_count = lax.axis_size("az")
    for i in range(z.az):
        for j in range(z.rng):
            pairs = [(a * az_count + b, c * az_count + d) for a, c in rng[j][2] for b, d in az[i][2]]
            rim.append(lax.ppermute(packed[z.az + z.rng + i * z.rng + j], ("rng", "az"), pairs))
    rim, _ = lax.optimization_barrier((rim, columns))
    rim = jnp.concatenate(rim, axis=1)
    field = shape((z.dates, z.lines, z.cols), F32)
    out = shape((z.dates, z.slots, z.lines, z.cols), BF16)
    own, mean, inv, log, part, bundle = pl.pallas_call(
        lambda *refs: stats_kernel(z, *refs),
        out_shape=[shape((z.images, z.rows, z.width), BF16), field, field, field, shape((z.lines, z.cols), BF16)]
        + [shape((rim.shape[0], z.rim_width + z.cols * (z.lines // STRIP)), BF16)],
        in_specs=vmem(3),
        out_specs=vmem(6),
        compiler_params=PARAMS,
        cost_estimate=COST,
        name="stats",
    )(held, rim, columns)

    rotated = 2 < count <= 4
    if rotated:
        later_rim = lax.ppermute(bundle, "date", [(i, (i - 1) % count) for i in range(count)])
        parts = [part]
        for k in range(2, count):
            parts.append(lax.ppermute(part, "date", [(i, (i - k) % count) for i in range(count)]))
    else:
        later_rim = lax.ppermute(rim, "date", earlier)
        parts = [lax.psum(part, "date")]

    coherence, log_ratio = pl.pallas_call(
        lambda *refs: own_kernel(z, *refs),
        out_shape=[out, out],
        in_specs=vmem(5),
        out_specs=vmem(2),
        scratch_shapes=[own_lists, pltpu.SemaphoreType.DMA],
        compiler_params=PARAMS,
        cost_estimate=COST,
        name="own",
    )(lists, columns, own, inv, log)
    other, held_out = pltpu.VMEM(field.shape, F32), pltpu.VMEM(out.shape, BF16)
    last = shape((z.dates - z.ends[-1],) + out.shape[1:], BF16)
    coherence, log_ratio, coh_last, log_last = pl.pallas_call(
        lambda *refs: cross_kernel(z, *refs),
        out_shape=[out, out, last, last],
        in_specs=vmem(9),
        out_specs=[HBM] * 2 + vmem(2),
        scratch_shapes=[pltpu.VMEM((z.images, z.rows, z.width), BF16), other, other, own_lists, held_out, held_out]
        + [pltpu.SemaphoreType.DMA((4,))],
        compiler_params=PARAMS,
        cost_estimate=COST,
        name="cross",
    )(later, later_rim, lists, columns, own, inv, log, coherence, log_ratio)
    return pl.pallas_call(
        lambda *refs: quegan_kernel(z, z.dates * count, rotated, *refs),
        out_shape=(out, out, field),
        in_specs=[HBM] * 2 + vmem(4 + len(parts)),
        out_specs=(HBM, HBM, HBM),
        scratch_shapes=[pltpu.VMEM(field.shape, F32), pltpu.SemaphoreType.DMA((3,))],
        input_output_aliases={0: 0, 1: 1},
        compiler_params=PARAMS,
        cost_estimate=COST,
        name="quegan",
    )(coherence, log_ratio, coh_last, log_last, mean, later_rim, *parts)


def solution(mesh):
    return jax.shard_map(
        on_device,
        mesh=mesh,
        in_specs=(P(("slab", "date"), None, "az", "rng"), P("date", None)),
        out_specs=(
            P(("slab", "date"), None, "az", "rng"),
            P(("slab", "date"), None, "az", "rng"),
            P(("slab", "date"), "az", "rng"),
        ),
        check_vma=False,
    )
```

profile of v0, /device:TPU:0, one launch (start us, length us, event | category | flops | bytes accessed | tf_op | source)
XLA Modules:
  0.0 24.7 jit_solution(12647120856830004283)
XLA Ops:
  0.6 1.3 %collective-permute-start = (bf16[1024,256]{1,0:T(8,128)(2,1)}, bf16[1024,256]{1,0:T(8,128)(2,1)S(1)}, u32[]{:S(2)}, u32[]{:S(2)}) collective-permute-start(bf16[1024,256]{1,0:T(8,128)(2,1)} %bitcast.1), channel_id=1, source_target_pairs={{4,0},{8,4},{12,8},{5,1},{9,5},{13,9},{6,2},{10,6},{14,10},{7,3},{... | collective-permute-start | bytes 1572872 | tf_op jit(solution)/shard_map/ppermute | solution.py:342
  1.9 1.4 %pack.1 = (bf16[16,512]{1,0:T(8,128)(2,1)S(1)}, bf16[16,1024]{1,0:T(8,128)(2,1)S(1)}, bf16[16,128]{1,0:T(8,128)(2,1)S(1)}, bf16[1024,256]{1,0:T(8,128)(2,1)S(1)}) custom-call(bf16[1024,256]{1,0:T(8,128)(2,1)} %bitcast.2), custom_call_target="tpu_custom_call" | custom-call | flops 1 | bytes 1 | tf_op jit(solution)/shard_map/pack/pallas_call | solution.py:343
  3.4 3.0 %collective-permute-start.2 = (bf16[16,1024]{1,0:T(8,128)(2,1)S(1)}, bf16[16,1024]{1,0:T(8,128)(2,1)S(1)}, u32[]{:S(2)}, u32[]{:S(2)}) collective-permute-start(bf16[16,1024]{1,0:T(8,128)(2,1)S(1)} %get-tuple-element.27), channel_id=1, source_target_pairs={{0,2},{2,0},{1,3},{3,1},{4,6},{6,4},{5,7},{7,5},{8,10},{10,8},{9,1... | collective-permute-start | bytes 98312 | tf_op jit(solution)/shard_map/ppermute | solution.py:374
  6.4 0.0 collective-permute-start.1
  6.4 0.2 collective-permute-start.3
  6.6 1.6 %prepare.1 = (bf16[384,256]{1,0:T(8,128)(2,1)S(1)}, s32[3,49]{1,0:T(4,128)S(1)}) custom-call(s32[8,6]{1,0:T(8,128)} %refs_0_), custom_call_target="tpu_custom_call" | custom-call | flops 1 | bytes 1 | tf_op jit(solution)/shard_map/prepare/pallas_call | solution.py:363
  8.2 1.2 %collective-permute-done.3 = bf16[16,128]{1,0:T(8,128)(2,1)S(1)} collective-permute-done((bf16[16,128]{1,0:T(8,128)(2,1)S(1)}, bf16[16,128]{1,0:T(8,128)(2,1)S(1)}, u32[]{:S(2)}, u32[]{:S(2)}) %collective-permute-start.3) | collective-permute-done | bytes 4128 | tf_op jit(solution)/shard_map/ppermute | solution.py:379
  9.4 0.0 collective-permute-done.1
  9.4 0.0 collective-permute-done.2
  9.4 1.1 %stats.1 = (bf16[16,80,384]{2,1,0:T(8,128)(2,1)S(1)}, f32[8,64,256]{2,1,0:T(8,128)S(1)}, f32[8,64,256]{2,1,0:T(8,128)S(1)}, f32[8,64,256]{2,1,0:T(8,128)S(1)}, b...) custom-call(bf16[1024,256]{1,0:T(8,128)(2,1)S(1)} %get-tuple-element.25.refs_0_, ...), custom_call_target="tpu_custom_call" | custom-call | flops 1 | bytes 1 | tf_op jit(solution)/shard_map/stats/pallas_call | solution.py:384
  10.5 4.8 %collective-permute-start.4 = (bf16[16,2688]{1,0:T(8,128)(2,1)S(1)}, bf16[16,2688]{1,0:T(8,128)(2,1)S(1)}, u32[]{:S(2)}, u32[]{:S(2)}) collective-permute-start(bf16[16,2688]{1,0:T(8,128)(2,1)S(1)} %get-tuple-element.34), channel_id=1, source_target_pairs={{0,12},{4,0},{8,4},{12,8},{1,13},{5,1},{9,5},{13,9},{2,14},{6,2},{... | collective-permute-start | bytes 258056 | tf_op jit(solution)/shard_map/ppermute | solution.py:397
  15.3 0.0 collective-permute-start.5
  15.3 1.0 %collective-permute-start.6 = (bf16[64,256]{1,0:T(8,128)(2,1)S(1)}, bf16[64,256]{1,0:T(8,128)(2,1)S(1)}, u32[]{:S(2)}, u32[]{:S(2)}) collective-permute-start(bf16[64,256]{1,0:T(8,128)(2,1)S(1)} %get-tuple-element.46.refs_6_), channel_id=1, source_target_pairs={{0,4},{4,8},{8,12},{12,0},{1,5},{5,9},{9,13},{13,1},{2,6},{6,10},{... | collective-permute-start | bytes 98312 | tf_op jit(solution)/shard_map/ppermute | solution.py:400
  16.3 3.0 %own.1 = (bf16[8,6,64,256]{3,2,1,0:T(8,128)(2,1)S(1)}, bf16[8,6,64,256]{3,2,1,0:T(8,128)(2,1)S(1)}) custom-call(s32[3,49]{1,0:T(4,128)S(1)} %get-tuple-element.35.refs_0_.refs_2_, bf16[384,256]{1,0:T(8,128)(2,1)S(1)} %get-tuple-element.30.refs_2_.refs_1_.refs_3_, bf16[16,80,384]{2,1,0:T(8,128)(2,1)S(1)} %get-tuple-element.36.refs_2_.refs_4_, ...), custom_call_target="tpu_custom_call" | custom-call | flops 1 | bytes 1 | tf_op jit(solution)/shard_map/own/pallas_call | solution.py:405
  19.3 0.3 %collective-permute-done.4.refs_1_.refs_5_ = bf16[16,2688]{1,0:T(8,128)(2,1)S(1)} collective-permute-done((bf16[16,2688]{1,0:T(8,128)(2,1)S(1)}, bf16[16,2688]{1,0:T(8,128)(2,1)S(1)}, u32[]{:S(2)}, u32[]{:S(2)}) %collective-permute-start.4) | collective-permute-done | bytes 86048 | tf_op jit(solution)/shard_map/ppermute | solution.py:397
  19.5 0.0 collective-permute-done.refs_0_
  19.5 3.9 %cross.1 = (bf16[8,6,64,256]{3,2,1,0:T(8,128)(2,1)}, bf16[8,6,64,256]{3,2,1,0:T(8,128)(2,1)}, bf16[3,6,64,256]{3,2,1,0:T(8,128)(2,1)S(1)}, bf16[3,6,64,256]{3,2,1,0:T(8,128)(2,1)S(1)}) custom-call(bf16[1024,256]{1,0:T(8,128)(2,1)S(1)} %collective-permute-done.refs_0_, bf16[16,2688]{1,0:T(8,128)(2,1)S(1)} %collective-permute-done.4.refs_1_.refs_5_, ...), custom_call_target="tpu_custom_call" | custom-call | flops 1 | bytes 1 | tf_op jit(solution)/shard_map/cross/pallas_call | solution.py:417
  23.5 0.0 collective-permute-done.5.refs_7_
  23.5 0.0 collective-permute-done.6.refs_8_
  23.5 1.2 %quegan.1 = (bf16[8,6,64,256]{3,2,1,0:T(8,128)(2,1)}, bf16[8,6,64,256]{3,2,1,0:T(8,128)(2,1)}, f32[8,64,256]{2,1,0:T(8,128)}) custom-call(bf16[8,6,64,256]{3,2,1,0:T(8,128)(2,1)} %get-tuple-element.41.refs_0_, bf16[8,6,64,256]{3,2,1,0:T(8,128)(2,1)} %get-tuple-element.42.refs_1_, ...), custom_call_target="tpu_custom_call", output_to_operand_aliasing={{0}: (0, {}), {1}: (1, {})} | custom-call | flops 1 | bytes 1 | tf_op jit(solution)/shard_map/quegan/pallas_call | solution.py:428
  (1 shorter events, 0.0 us)
Async XLA Ops:
  0.6 18.9 %collective-permute-start = (bf16[1024,256]{1,0:T(8,128)(2,1)}, bf16[1024,256]{1,0:T(8,128)(2,1)S(1)}, u32[]{:S(2)}, u32[]{:S(2)}) collective-permute-start(bf16[1024,256]{1,0:T(8,128)(2,1)} %bitcast.1), channel_id=1, source_target_pairs={{4,0},{8,4},{12,8},{5,1},{9,5},{13,9},{6,2},{10,6},{14,10},{7,3},{... | collective-permute-start | bytes 1572872 | tf_op jit(solution)/shard_map/ppermute | solution.py:342
  3.4 6.0 %collective-permute-start.2 = (bf16[16,1024]{1,0:T(8,128)(2,1)S(1)}, bf16[16,1024]{1,0:T(8,128)(2,1)S(1)}, u32[]{:S(2)}, u32[]{:S(2)}) collective-permute-start(bf16[16,1024]{1,0:T(8,128)(2,1)S(1)} %get-tuple-element.27), channel_id=1, source_target_pairs={{0,2},{2,0},{1,3},{3,1},{4,6},{6,4},{5,7},{7,5},{8,10},{10,8},{9,1... | collective-permute-start | bytes 98312 | tf_op jit(solution)/shard_map/ppermute | solution.py:374
  6.4 3.0 %collective-permute-start.1 = (bf16[16,512]{1,0:T(8,128)(2,1)S(1)}, bf16[16,512]{1,0:T(8,128)(2,1)S(1)}, u32[]{:S(2)}, u32[]{:S(2)}) collective-permute-start(bf16[16,512]{1,0:T(8,128)(2,1)S(1)} %get-tuple-element.26), channel_id=1, source_target_pairs={{0,1},{1,0},{2,3},{3,2},{4,5},{5,4},{6,7},{7,6},{8,9},{9,8},{10,11... | collective-permute-start | bytes 49160 | tf_op jit(solution)/shard_map/ppermute | solution.py:361
  6.4 3.0 %collective-permute-start.3 = (bf16[16,128]{1,0:T(8,128)(2,1)S(1)}, bf16[16,128]{1,0:T(8,128)(2,1)S(1)}, u32[]{:S(2)}, u32[]{:S(2)}) collective-permute-start(bf16[16,128]{1,0:T(8,128)(2,1)S(1)} %get-tuple-element.28), channel_id=1, source_target_pairs={{0,3},{1,2},{2,1},{3,0},{4,7},{5,6},{6,5},{7,4},{8,11},{9,10},{10,... | collective-permute-start | bytes 12296 | tf_op jit(solution)/shard_map/ppermute | solution.py:379
  10.5 9.0 %collective-permute-start.4 = (bf16[16,2688]{1,0:T(8,128)(2,1)S(1)}, bf16[16,2688]{1,0:T(8,128)(2,1)S(1)}, u32[]{:S(2)}, u32[]{:S(2)}) collective-permute-start(bf16[16,2688]{1,0:T(8,128)(2,1)S(1)} %get-tuple-element.34), channel_id=1, source_target_pairs={{0,12},{4,0},{8,4},{12,8},{1,13},{5,1},{9,5},{13,9},{2,14},{6,2},{... | collective-permute-start | bytes 258056 | tf_op jit(solution)/shard_map/ppermute | solution.py:397
  15.3 8.2 %collective-permute-start.5 = (bf16[64,256]{1,0:T(8,128)(2,1)S(1)}, bf16[64,256]{1,0:T(8,128)(2,1)S(1)}, u32[]{:S(2)}, u32[]{:S(2)}) collective-permute-start(bf16[64,256]{1,0:T(8,128)(2,1)S(1)} %get-tuple-element.46.refs_6_), channel_id=1, source_target_pairs={{0,8},{4,12},{8,0},{12,4},{1,9},{5,13},{9,1},{13,5},{2,10},{6,14},... | collective-permute-start | bytes 98312 | tf_op jit(solution)/shard_map/ppermute | solution.py:400
  15.3 8.2 %collective-permute-start.6 = (bf16[64,256]{1,0:T(8,128)(2,1)S(1)}, bf16[64,256]{1,0:T(8,128)(2,1)S(1)}, u32[]{:S(2)}, u32[]{:S(2)}) collective-permute-start(bf16[64,256]{1,0:T(8,128)(2,1)S(1)} %get-tuple-element.46.refs_6_), channel_id=1, source_target_pairs={{0,4},{4,8},{8,12},{12,0},{1,5},{5,9},{9,13},{13,1},{2,6},{6,10},{... | collective-permute-start | bytes 98312 | tf_op jit(solution)/shard_map/ppermute | solution.py:400
where the time goes:
time: 24.8 us; the launch traced here: 24.7 us
  Pallas kernels  12.3 us (50%)
  starting transfers between devices  10.2 us (41%)
  waiting for transfers between devices  1.51 us (6%)
  between operations  0.7 us (3%)
    ppermute x1, starting transfers between devices, on_device(): lax.ppermute(bundle, 'date', [(i, (i - 1) % count) for i in range(count)])  4.77 us
    pallas_call x1, Pallas kernels, on_device(): pl.pallas_call(lambda *refs: cross_kernel(z, *refs), out_shape=[out, out,...  3.94 us
    ppermute x1, starting transfers between devices, on_device(): lax.ppermute(packed[z.az + j], 'rng', rng[j][2])  3 us
    pallas_call x1, Pallas kernels, on_device(): pl.pallas_call(lambda *refs: own_kernel(z, *refs), out_shape=[out, out],...  2.99 us
    pallas_call x1, Pallas kernels, on_device(): pl.pallas_call(lambda *refs: prepare_kernel(z, *refs), out_shape=[shape((...  1.58 us
    pallas_call x1, Pallas kernels, on_device(): pl.pallas_call(lambda *refs: pack_kernel(z, *refs), out_shape=[shape((STR...  1.43 us
    ppermute x1, starting transfers between devices, on_device(): later = lax.ppermute(flat, 'date', earlier)  1.29 us
    ppermute x1, waiting for transfers between devices, on_device(): lax.ppermute(packed[z.az + z.rng + i * z.rng + j], ('rng', 'az'), pairs)  1.24 us
  transfers between devices with their start and end apart: 7, of which 2 were waited for; matrix products, arithmetic and copies ran while one was open for 0% of the time, Pallas kernels for 45%

commit v1 on v0

--- a/solution.py
+++ b/solution.py
@@ -14,7 +14,8 @@
 F32 = jnp.float32
 STRIP = 16
 LANES = 128
-GROUP = 4
+GROUP = 5
+BATCH = 4
 ENDS = (3, 5)
 PARTS = 1
 
@@ -195,8 +196,8 @@
 def stats_kernel(z, x_ref, rim_ref, columns, tile_ref, mean_ref, inv_ref, log_ref, part_ref, bundle_ref):
     assemble(z, tile_ref, x_ref, rim_ref, 0, z.images)
     part = jnp.zeros((z.lines, z.cols), F32)
-    for first in range(0, z.dates, GROUP):
-        for d, power, mean, inv in look_stats(z, tile_ref, first, min(GROUP, z.dates - first), columns[...]):
+    for first in range(0, z.dates, BATCH):
+        for d, power, mean, inv in look_stats(z, tile_ref, first, min(BATCH, z.dates - first), columns[...]):
             mean_ref[d] = mean
             inv_ref[d] = inv * (1.0 / LOOKS)
             log_ref[d] = jnp.log(mean)
@@ -267,8 +268,8 @@
     for take in takes:
         take.start()
     assemble(z, tile, x_ref, rim_ref, 0, z.images)
-    for first in range(0, z.dates, GROUP):
-        for d, _, mean, inverse in look_stats(z, tile, first, min(GROUP, z.dates - first), columns[...]):
+    for first in range(0, z.dates, BATCH):
+        for d, _, mean, inverse in look_stats(z, tile, first, min(BATCH, z.dates - first), columns[...]):
             inv[d] = inverse * (1.0 / LOOKS)
             log[d] = jnp.log(mean)
     for take in takes:

time: 24.8 us -> 24.9 us (level); the launches traced: 24.7 us -> 24.5 us
  waiting for transfers between devices: 1.51 us -> 1.25 us
    pallas_call x1, Pallas kernels: 3.94 us -> 3.41 us  [on_device(): pl.pallas_call(lambda *refs: cross_kernel(z, *refs), out_shape=[out, out,...]
    pallas_call x1, Pallas kernels: 2.99 us -> 3.52 us  [on_device(): pl.pallas_call(lambda *refs: own_kernel(z, *refs), out_shape=[out, out],...]
    ppermute x1, waiting for transfers between devices: 0.26 us -> 0.01 us  [on_device(): lax.ppermute(bundle, 'date', [(i, (i - 1) % count) for i in range(count)])]
  transfers between devices with their start and end apart: 7 -> 7, of which waited for: 2 -> 1; matrix products, arithmetic and copies ran while one was open for 0% -> 0% of each run, Pallas kernels for 45% -> 45%
where the time goes in v1:
time: 24.9 us; the launch traced here: 24.5 us
  Pallas kernels  12.3 us (49%)
  starting transfers between devices  10.2 us (41%)
  waiting for transfers between devices  1.25 us (5%)
  between operations  0.72 us (3%)
    ppermute x1, starting transfers between devices, on_device(): lax.ppermute(bundle, 'date', [(i, (i - 1) % count) for i in range(count)])  4.77 us
    pallas_call x1, Pallas kernels, on_device(): pl.pallas_call(lambda *refs: own_kernel(z, *refs), out_shape=[out, out],...  3.52 us
    pallas_call x1, Pallas kernels, on_device(): pl.pallas_call(lambda *refs: cross_kernel(z, *refs), out_shape=[out, out,...  3.41 us
    ppermute x1, starting transfers between devices, on_device(): lax.ppermute(packed[z.az + j], 'rng', rng[j][2])  3 us
    pallas_call x1, Pallas kernels, on_device(): pl.pallas_call(lambda *refs: prepare_kernel(z, *refs), out_shape=[shape((...  1.58 us
    pallas_call x1, Pallas kernels, on_device(): pl.pallas_call(lambda *refs: pack_kernel(z, *refs), out_shape=[shape((STR...  1.43 us
    ppermute x1, starting transfers between devices, on_device(): later = lax.ppermute(flat, 'date', earlier)  1.29 us
    ppermute x1, waiting for transfers between devices, on_device(): lax.ppermute(packed[z.az + z.rng + i * z.rng + j], ('rng', 'az'), pairs)  1.24 us
  transfers between devices with their start and end apart: 7, of which 1 were waited for; matrix products, arithmetic and copies ran while one was open for 0% of the time, Pallas kernels for 45%

profile of v1, /device:TPU:0, one launch (start us, length us, event | category | flops | bytes accessed | tf_op | source)
XLA Modules:
  0.0 24.5 jit_solution(3520317768853136242)
XLA Ops:
  0.6 1.3 %collective-permute-start = (bf16[1024,256]{1,0:T(8,128)(2,1)}, bf16[1024,256]{1,0:T(8,128)(2,1)S(1)}, u32[]{:S(2)}, u32[]{:S(2)}) collective-permute-start(bf16[1024,256]{1,0:T(8,128)(2,1)} %bitcast.1), channel_id=1, source_target_pairs={{4,0},{8,4},{12,8},{5,1},{9,5},{13,9},{6,2},{10,6},{14,10},{7,3},{... | collective-permute-start | bytes 1572872 | tf_op jit(solution)/shard_map/ppermute | solution.py:343
  1.9 1.4 %pack.1 = (bf16[16,512]{1,0:T(8,128)(2,1)S(1)}, bf16[16,1024]{1,0:T(8,128)(2,1)S(1)}, bf16[16,128]{1,0:T(8,128)(2,1)S(1)}, bf16[1024,256]{1,0:T(8,128)(2,1)S(1)}) custom-call(bf16[1024,256]{1,0:T(8,128)(2,1)} %bitcast.2), custom_call_target="tpu_custom_call" | custom-call | flops 1 | bytes 1 | tf_op jit(solution)/shard_map/pack/pallas_call | solution.py:344
  3.4 3.0 %collective-permute-start.2 = (bf16[16,1024]{1,0:T(8,128)(2,1)S(1)}, bf16[16,1024]{1,0:T(8,128)(2,1)S(1)}, u32[]{:S(2)}, u32[]{:S(2)}) collective-permute-start(bf16[16,1024]{1,0:T(8,128)(2,1)S(1)} %get-tuple-element.27), channel_id=1, source_target_pairs={{0,2},{2,0},{1,3},{3,1},{4,6},{6,4},{5,7},{7,5},{8,10},{10,8},{9,1... | collective-permute-start | bytes 98312 | tf_op jit(solution)/shard_map/ppermute | solution.py:375
  6.4 0.0 collective-permute-start.1
  6.4 0.2 collective-permute-start.3
  6.6 1.6 %prepare.1 = (bf16[384,256]{1,0:T(8,128)(2,1)S(1)}, s32[3,49]{1,0:T(4,128)S(1)}) custom-call(s32[8,6]{1,0:T(8,128)} %refs_0_), custom_call_target="tpu_custom_call" | custom-call | flops 1 | bytes 1 | tf_op jit(solution)/shard_map/prepare/pallas_call | solution.py:364
  8.2 1.2 %collective-permute-done.3 = bf16[16,128]{1,0:T(8,128)(2,1)S(1)} collective-permute-done((bf16[16,128]{1,0:T(8,128)(2,1)S(1)}, bf16[16,128]{1,0:T(8,128)(2,1)S(1)}, u32[]{:S(2)}, u32[]{:S(2)}) %collective-permute-start.3) | collective-permute-done | bytes 4128 | tf_op jit(solution)/shard_map/ppermute | solution.py:380
  9.4 0.0 collective-permute-done.1
  9.4 0.0 collective-permute-done.2
  9.4 1.1 %stats.1 = (bf16[16,80,384]{2,1,0:T(8,128)(2,1)S(1)}, f32[8,64,256]{2,1,0:T(8,128)S(1)}, f32[8,64,256]{2,1,0:T(8,128)S(1)}, f32[8,64,256]{2,1,0:T(8,128)S(1)}, b...) custom-call(bf16[1024,256]{1,0:T(8,128)(2,1)S(1)} %get-tuple-element.25.refs_0_, ...), custom_call_target="tpu_custom_call" | custom-call | flops 1 | bytes 1 | tf_op jit(solution)/shard_map/stats/pallas_call | solution.py:385
  10.5 4.8 %collective-permute-start.4 = (bf16[16,2688]{1,0:T(8,128)(2,1)S(1)}, bf16[16,2688]{1,0:T(8,128)(2,1)S(1)}, u32[]{:S(2)}, u32[]{:S(2)}) collective-permute-start(bf16[16,2688]{1,0:T(8,128)(2,1)S(1)} %get-tuple-element.34), channel_id=1, source_target_pairs={{0,12},{4,0},{8,4},{12,8},{1,13},{5,1},{9,5},{13,9},{2,14},{6,2},{... | collective-permute-start | bytes 258056 | tf_op jit(solution)/shard_map/ppermute | solution.py:398
  15.3 0.0 collective-permute-start.5
  15.3 1.0 %collective-permute-start.6 = (bf16[64,256]{1,0:T(8,128)(2,1)S(1)}, bf16[64,256]{1,0:T(8,128)(2,1)S(1)}, u32[]{:S(2)}, u32[]{:S(2)}) collective-permute-start(bf16[64,256]{1,0:T(8,128)(2,1)S(1)} %get-tuple-element.46.refs_6_), channel_id=1, source_target_pairs={{0,4},{4,8},{8,12},{12,0},{1,5},{5,9},{9,13},{13,1},{2,6},{6,10},{... | collective-permute-start | bytes 98312 | tf_op jit(solution)/shard_map/ppermute | solution.py:401
  16.3 3.5 %own.1 = (bf16[8,6,64,256]{3,2,1,0:T(8,128)(2,1)S(1)}, bf16[8,6,64,256]{3,2,1,0:T(8,128)(2,1)S(1)}) custom-call(s32[3,49]{1,0:T(4,128)S(1)} %get-tuple-element.35.refs_0_.refs_2_, bf16[384,256]{1,0:T(8,128)(2,1)S(1)} %get-tuple-element.30.refs_2_.refs_1_.refs_3_, bf16[16,80,384]{2,1,0:T(8,128)(2,1)S(1)} %get-tuple-element.36.refs_2_.refs_4_, ...), custom_call_target="tpu_custom_call" | custom-call | flops 1 | bytes 1 | tf_op jit(solution)/shard_map/own/pallas_call | solution.py:406
  19.8 0.0 collective-permute-done.4.refs_1_.refs_5_
  19.8 0.0 collective-permute-done.refs_0_
  19.8 3.4 %cross.1 = (bf16[8,6,64,256]{3,2,1,0:T(8,128)(2,1)}, bf16[8,6,64,256]{3,2,1,0:T(8,128)(2,1)}, bf16[3,6,64,256]{3,2,1,0:T(8,128)(2,1)S(1)}, bf16[3,6,64,256]{3,2,1,0:T(8,128)(2,1)S(1)}) custom-call(bf16[1024,256]{1,0:T(8,128)(2,1)S(1)} %collective-permute-done.refs_0_, bf16[16,2688]{1,0:T(8,128)(2,1)S(1)} %collective-permute-done.4.refs_1_.refs_5_, ...), custom_call_target="tpu_custom_call" | custom-call | flops 1 | bytes 1 | tf_op jit(solution)/shard_map/cross/pallas_call | solution.py:418
  23.2 0.0 collective-permute-done.5.refs_7_
  23.2 0.0 collective-permute-done.6.refs_8_
  23.3 1.2 %quegan.1 = (bf16[8,6,64,256]{3,2,1,0:T(8,128)(2,1)}, bf16[8,6,64,256]{3,2,1,0:T(8,128)(2,1)}, f32[8,64,256]{2,1,0:T(8,128)}) custom-call(bf16[8,6,64,256]{3,2,1,0:T(8,128)(2,1)} %get-tuple-element.41.refs_0_, bf16[8,6,64,256]{3,2,1,0:T(8,128)(2,1)} %get-tuple-element.42.refs_1_, ...), custom_call_target="tpu_custom_call", output_to_operand_aliasing={{0}: (0, {}), {1}: (1, {})} | custom-call | flops 1 | bytes 1 | tf_op jit(solution)/shard_map/quegan/pallas_call | solution.py:429
  (1 shorter events, 0.0 us)
Async XLA Ops:
  0.6 19.2 %collective-permute-start = (bf16[1024,256]{1,0:T(8,128)(2,1)}, bf16[1024,256]{1,0:T(8,128)(2,1)S(1)}, u32[]{:S(2)}, u32[]{:S(2)}) collective-permute-start(bf16[1024,256]{1,0:T(8,128)(2,1)} %bitcast.1), channel_id=1, source_target_pairs={{4,0},{8,4},{12,8},{5,1},{9,5},{13,9},{6,2},{10,6},{14,10},{7,3},{... | collective-permute-start | bytes 1572872 | tf_op jit(solution)/shard_map/ppermute | solution.py:343
  3.4 6.0 %collective-permute-start.2 = (bf16[16,1024]{1,0:T(8,128)(2,1)S(1)}, bf16[16,1024]{1,0:T(8,128)(2,1)S(1)}, u32[]{:S(2)}, u32[]{:S(2)}) collective-permute-start(bf16[16,1024]{1,0:T(8,128)(2,1)S(1)} %get-tuple-element.27), channel_id=1, source_target_pairs={{0,2},{2,0},{1,3},{3,1},{4,6},{6,4},{5,7},{7,5},{8,10},{10,8},{9,1... | collective-permute-start | bytes 98312 | tf_op jit(solution)/shard_map/ppermute | solution.py:375
  6.4 3.0 %collective-permute-start.1 = (bf16[16,512]{1,0:T(8,128)(2,1)S(1)}, bf16[16,512]{1,0:T(8,128)(2,1)S(1)}, u32[]{:S(2)}, u32[]{:S(2)}) collective-permute-start(bf16[16,512]{1,0:T(8,128)(2,1)S(1)} %get-tuple-element.26), channel_id=1, source_target_pairs={{0,1},{1,0},{2,3},{3,2},{4,5},{5,4},{6,7},{7,6},{8,9},{9,8},{10,11... | collective-permute-start | bytes 49160 | tf_op jit(solution)/shard_map/ppermute | solution.py:362
  6.4 3.0 %collective-permute-start.3 = (bf16[16,128]{1,0:T(8,128)(2,1)S(1)}, bf16[16,128]{1,0:T(8,128)(2,1)S(1)}, u32[]{:S(2)}, u32[]{:S(2)}) collective-permute-start(bf16[16,128]{1,0:T(8,128)(2,1)S(1)} %get-tuple-element.28), channel_id=1, source_target_pairs={{0,3},{1,2},{2,1},{3,0},{4,7},{5,6},{6,5},{7,4},{8,11},{9,10},{10,... | collective-permute-start | bytes 12296 | tf_op jit(solution)/shard_map/ppermute | solution.py:380
  10.5 9.3 %collective-permute-start.4 = (bf16[16,2688]{1,0:T(8,128)(2,1)S(1)}, bf16[16,2688]{1,0:T(8,128)(2,1)S(1)}, u32[]{:S(2)}, u32[]{:S(2)}) collective-permute-start(bf16[16,2688]{1,0:T(8,128)(2,1)S(1)} %get-tuple-element.34), channel_id=1, source_target_pairs={{0,12},{4,0},{8,4},{12,8},{1,13},{5,1},{9,5},{13,9},{2,14},{6,2},{... | collective-permute-start | bytes 258056 | tf_op jit(solution)/shard_map/ppermute | solution.py:398
  15.3 7.9 %collective-permute-start.5 = (bf16[64,256]{1,0:T(8,128)(2,1)S(1)}, bf16[64,256]{1,0:T(8,128)(2,1)S(1)}, u32[]{:S(2)}, u32[]{:S(2)}) collective-permute-start(bf16[64,256]{1,0:T(8,128)(2,1)S(1)} %get-tuple-element.46.refs_6_), channel_id=1, source_target_pairs={{0,8},{4,12},{8,0},{12,4},{1,9},{5,13},{9,1},{13,5},{2,10},{6,14},... | collective-permute-start | bytes 98312 | tf_op jit(solution)/shard_map/ppermute | solution.py:401
  15.3 7.9 %collective-permute-start.6 = (bf16[64,256]{1,0:T(8,128)(2,1)S(1)}, bf16[64,256]{1,0:T(8,128)(2,1)S(1)}, u32[]{:S(2)}, u32[]{:S(2)}) collective-permute-start(bf16[64,256]{1,0:T(8,128)(2,1)S(1)} %get-tuple-element.46.refs_6_), channel_id=1, source_target_pairs={{0,4},{4,8},{8,12},{12,0},{1,5},{5,9},{9,13},{13,1},{2,6},{6,10},{... | collective-permute-start | bytes 98312 | tf_op jit(solution)/shard_map/ppermute | solution.py:401
